TPU v7x, 256 devices: a whole 4x4x8 slice. The times are simulated.
256 devices in a mesh: node: 16 (over y, x), local: 16 (over z, core).
Axes of the slice: x: 4, y: 4, z: 8, core: 2. Of those that a mesh axis runs over, the one named last changes fastest.
Arguments:
- inputs: bfloat16 [16384, 3584], P(('node', 'local')), may hold values from -6 to 6
- out_grad: bfloat16 [16384, 3584], P(('node', 'local')), may hold values from -6 to 6
- experts: int32 [16384, 2], P(('node', 'local')), may hold values from 0 to 127, as said below
- gate_values: bfloat16 [16384, 2], P(('node', 'local')), may hold values from 0.049804688 to 0.59765625
- gate_matrix: bfloat16 [256, 3584, 512], P(('node', 'local')), may hold values from -0.09375 to 0.09375
- up_matrix: bfloat16 [256, 3584, 512], P(('node', 'local')), may hold values from -0.09375 to 0.09375
- down_matrix: bfloat16 [256, 512, 3584], P(('node', 'local')), may hold values from -0.1875 to 0.1875
Outputs:
- input_grad: bfloat16 [16384, 3584], P(('node', 'local'))
Inputs may be any that keep to these rules, and one draw needn't show every extreme that they name: Each token names 2 different experts, and both lie on the same node. Of the tokens of one device, at most 8 use one node and at most 2 name one expert; in every draw one node is used by exactly 8 tokens of every device, and each of its experts is named by exactly 2 tokens of every device.
All inputs are finite; a program needn't handle non-finite values.
Results may differ from a plain program's by a relative error of at most 0.0057.
Values may be sent and summed in bfloat16 or wider, within the bound.
A program may use at most 128 MiB of HBM per device.

v0:
```python
import jax
import jax.numpy as jnp
from jax import lax
from jax.sharding import PartitionSpec as P

NODES_TOK = 1


def expert_rows(x_slots, grad_slots, gate_slots, gate_matrix, up_matrix, down_matrix):
    layout = x_slots.shape
    model_width = layout[-1]
    x_rows = x_slots.reshape(-1, model_width)
    grad_rows = grad_slots.reshape(-1, model_width)
    gate_rows = gate_slots.reshape(-1).astype(jnp.float32)
    w_gate = gate_matrix[0]
    w_up = up_matrix[0]
    w_down = down_matrix[0]
    contract_last = (((1,), (1,)), ((), ()))
    pre_gate = jnp.dot(x_rows, w_gate, preferred_element_type=jnp.float32)
    pre_up = jnp.dot(x_rows, w_up, preferred_element_type=jnp.float32)
    hidden_grad = gate_rows[:, None] * lax.dot_general(
        grad_rows, w_down, contract_last, preferred_element_type=jnp.float32
    )
    sig = jax.nn.sigmoid(pre_gate)
    grad_gate = (hidden_grad * pre_up * sig * (1.0 + pre_gate * (1.0 - sig))).astype(jnp.bfloat16)
    grad_up = (hidden_grad * pre_gate * sig).astype(jnp.bfloat16)
    result = lax.dot_general(grad_gate, w_gate, contract_last, preferred_element_type=jnp.float32)
    result = result + lax.dot_general(
        grad_up, w_up, contract_last, preferred_element_type=jnp.float32
    )
    return result.astype(jnp.bfloat16).reshape(layout)


def shards(inputs, out_grad, experts, gate_values, gate_matrix, up_matrix, down_matrix):
    node_count = lax.axis_size("node")
    local_count = lax.axis_size("local")
    per_node = local_count // 2
    tok_count, model_width = inputs.shape
    expert_count = node_count * per_node
    node_cap = min(tok_count, 2 * tok_count * NODES_TOK // node_count)
    slot_cap = 2 * node_cap // per_node
    expert_hits = experts[:, :, None] == jnp.arange(expert_count, dtype=jnp.int32)
    routed = jnp.any(expert_hits, axis=1).astype(jnp.int32)
    gate_table = jnp.sum(
        jnp.where(expert_hits, gate_values[:, :, None], jnp.zeros((), jnp.bfloat16)), axis=1
    )
    slot_rank = jnp.cumsum(routed, axis=0) - routed
    slot_pick = (routed[:, :, None] == 1) & (
        slot_rank[:, :, None] == jnp.arange(slot_cap, dtype=jnp.int32)
    )
    slot_select = jnp.transpose(slot_pick.astype(jnp.bfloat16), (1, 2, 0))
    gate_slot = jnp.sum(
        jnp.where(slot_pick, gate_table[:, :, None], jnp.zeros((), jnp.bfloat16)), axis=0
    )
    x_slots = jnp.einsum(
        "ect,td->ecd", slot_select, inputs, preferred_element_type=jnp.float32
    ).astype(jnp.bfloat16)
    grad_slots = jnp.einsum(
        "ect,td->ecd", slot_select, out_grad, preferred_element_type=jnp.float32
    ).astype(jnp.bfloat16)
    x_slots = jnp.repeat(x_slots.reshape(node_count, per_node, slot_cap, model_width), 2, axis=1)
    grad_slots = jnp.repeat(
        grad_slots.reshape(node_count, per_node, slot_cap, model_width), 2, axis=1
    )
    gate_slot = jnp.repeat(gate_slot.reshape(node_count, per_node, slot_cap), 2, axis=1)
    x_slots, grad_slots, gate_slot = (
        lax.all_to_all(x_slots, "node", split_axis=0, concat_axis=0, tiled=True),
        lax.all_to_all(grad_slots, "node", split_axis=0, concat_axis=0, tiled=True),
        lax.all_to_all(gate_slot, "node", split_axis=0, concat_axis=0, tiled=True),
    )
    x_slots, grad_slots, gate_slot = (
        lax.all_to_all(x_slots, "local", split_axis=1, concat_axis=1, tiled=True),
        lax.all_to_all(grad_slots, "local", split_axis=1, concat_axis=1, tiled=True),
        lax.all_to_all(gate_slot, "local", split_axis=1, concat_axis=1, tiled=True),
    )
    partials = expert_rows(x_slots, grad_slots, gate_slot, gate_matrix, up_matrix, down_matrix)
    returned = lax.all_to_all(partials, "local", split_axis=1, concat_axis=1, tiled=True)
    returned = lax.all_to_all(returned, "node", split_axis=0, concat_axis=0, tiled=True)
    select_half = jnp.repeat(
        slot_select.reshape(node_count, per_node, slot_cap, tok_count), 2, axis=1
    )
    node_sums = jnp.einsum(
        "mlct,mlcd->mtd", select_half, returned, preferred_element_type=jnp.float32
    ).astype(jnp.bfloat16)
    total = jnp.sum(node_sums.astype(jnp.float32), axis=0)
    return total.astype(jnp.bfloat16)


def solution(mesh):
    in_specs = (
        P(("node", "local"), None),
        P(("node", "local"), None),
        P(("node", "local"), None),
        P(("node", "local"), None),
        P(("node", "local"), None, None),
        P(("node", "local"), None, None),
        P(("node", "local"), None, None),
    )
    out_specs = P(("node", "local"), None)
    return jax.shard_map(shards, mesh=mesh, in_specs=in_specs, out_specs=out_specs, check_vma=False)
```

profile of v0, /device:TPU:1, one launch (start us, length us, event | category | flops | bytes accessed | tf_op | source)
XLA Modules:
  0.0 552.8 jit_solution(17811114455328504328)
XLA Ops:
  2.1 13.8 %all_to_all.40 = bf16[16,16,2]{1,2,0:T(2,128)(2,1)S(1)} all-to-all(bf16[16,16,2]{1,2,0:T(2,128)(2,1)S(1)} %copy.79), channel_id=1, replica_groups=mesh['node'=16,'local'=16] {'node'}, dimensions={0} | all-to-all | bytes 2048 | tf_op jit(solution)/shard_map/all_to_all | solution.py:69
  16.5 10.6 %all-to-all-start.1 = ((bf16[16,16,2]{0,2,1:T(2,128)(2,1)}), bf16[16,16,2]{0,2,1:T(2,128)(2,1)S(1)}, u32[]{:S(2)}, u32[]{:S(2)}) async-start(bf16[16,16,2]{0,2,1:T(2,128)(2,1)} %copy.80), calls=%async_computation.1 | async-start | bytes 16384 | tf_op jit(solution)/shard_map/all_to_all | solution.py:74
  27.8 1.9 copy.83
  29.7 4.4 all-to-all-done.1
  34.1 4.0 broadcast_in_dim.50
  38.0 4.6 all-to-all-start.2
  43.4 1.9 copy.86
  45.3 52.7 %all-to-all-done.2 = bf16[16,16,2,3584]{3,2,1,0:T(2,128)(2,1)} async-done(((bf16[16,16,2,3584]{3,2,1,0:T(2,128)(2,1)}), bf16[16,16,2,3584]{3,2,1,0:T(2,128)(2,1)}, u32[]{:S(2)}, u32[]{:S(2)}) %all-to-all-start.2) | async-done | bytes 3670048 | tf_op jit(solution)/shard_map/all_to_all | solution.py:68
  98.0 4.1 broadcast_in_dim.51
  102.0 4.8 all-to-all-start.4
  106.8 7.3 %copy.84 = bf16[16,16,2,3584]{3,2,0,1:T(2,128)(2,1)} copy(bf16[16,16,2,3584]{3,2,1,0:T(2,128)(2,1)} %all-to-all-done.2) | data formatting | bytes 7340032 | tf_op jit(solution)/shard_map/all_to_all | solution.py:68
  114.1 45.1 %all-to-all-done.4 = bf16[16,16,2,3584]{3,2,1,0:T(2,128)(2,1)} async-done(((bf16[16,16,2,3584]{3,2,1,0:T(2,128)(2,1)}), bf16[16,16,2,3584]{3,2,1,0:T(2,128)(2,1)}, u32[]{:S(2)}, u32[]{:S(2)}) %all-to-all-start.4) | async-done | bytes 3670048 | tf_op jit(solution)/shard_map/all_to_all | solution.py:67
  159.3 6.9 %all-to-all-start.3 = ((bf16[16,16,2,3584]{3,2,0,1:T(2,128)(2,1)}), bf16[16,16,2,3584]{3,2,0,1:T(2,128)(2,1)}, u32[]{:S(2)}, u32[]{:S(2)}) async-start(bf16[16,16,2,3584]{3,2,0,1:T(2,128)(2,1)} %copy.84), calls=%async_computation.3 | async-start | bytes 7340032 | tf_op jit(solution)/shard_map/all_to_all | solution.py:73
  166.1 7.2 %copy.87 = bf16[16,16,2,3584]{3,2,0,1:T(2,128)(2,1)} copy(bf16[16,16,2,3584]{3,2,1,0:T(2,128)(2,1)} %all-to-all-done.4) | data formatting | bytes 7340032 | tf_op jit(solution)/shard_map/all_to_all | solution.py:67
  173.3 75.2 %all-to-all-done.3 = bf16[16,16,2,3584]{3,2,0,1:T(2,128)(2,1)} async-done(((bf16[16,16,2,3584]{3,2,0,1:T(2,128)(2,1)}), bf16[16,16,2,3584]{3,2,0,1:T(2,128)(2,1)}, u32[]{:S(2)}, u32[]{:S(2)}) %all-to-all-start.3) | async-done | bytes 3670048 | tf_op jit(solution)/shard_map/all_to_all | solution.py:73
  248.5 6.2 %all-to-all-start.5 = ((bf16[16,16,2,3584]{3,2,0,1:T(2,128)(2,1)}), bf16[16,16,2,3584]{3,2,0,1:T(2,128)(2,1)}, u32[]{:S(2)}, u32[]{:S(2)}) async-start(bf16[16,16,2,3584]{3,2,0,1:T(2,128)(2,1)} %copy.87), calls=%async_computation.5 | async-start | bytes 7340032 | tf_op jit(solution)/shard_map/all_to_all | solution.py:72
  255.1 7.3 %copy.85 = bf16[16,16,2,3584]{3,2,1,0:T(2,128)(2,1)} copy(bf16[16,16,2,3584]{3,2,0,1:T(2,128)(2,1)} %all-to-all-done.3) | data formatting | bytes 7340032 | tf_op jit(solution)/shard_map/all_to_all | solution.py:73
  262.4 8.4 %reshape.65 = bf16[512,3584]{1,0:T(8,128)(2,1)} reshape(bf16[16,16,2,3584]{3,2,1,0:T(2,128)(2,1)} %copy.85) | data formatting | bytes 7340032 | tf_op jit(solution)/shard_map/reshape | solution.py:13
  270.8 66.1 %all-to-all-done.5 = bf16[16,16,2,3584]{3,2,0,1:T(2,128)(2,1)} async-done(((bf16[16,16,2,3584]{3,2,0,1:T(2,128)(2,1)}), bf16[16,16,2,3584]{3,2,0,1:T(2,128)(2,1)}, u32[]{:S(2)}, u32[]{:S(2)}) %all-to-all-start.5) | async-done | bytes 3670048 | tf_op jit(solution)/shard_map/all_to_all | solution.py:72
  336.9 7.2 %copy.88 = bf16[16,16,2,3584]{3,2,1,0:T(2,128)(2,1)} copy(bf16[16,16,2,3584]{3,2,0,1:T(2,128)(2,1)} %all-to-all-done.5) | data formatting | bytes 7340032 | tf_op jit(solution)/shard_map/all_to_all | solution.py:72
  344.1 8.5 %reshape.68 = bf16[512,3584]{1,0:T(8,128)(2,1)} reshape(bf16[16,16,2,3584]{3,2,1,0:T(2,128)(2,1)} %copy.88) | data formatting | bytes 7340032 | tf_op jit(solution)/shard_map/reshape | solution.py:12
  352.6 5.3 fusion.4
  358.0 2.1 fusion.12
  360.1 11.3 %fusion.2 = f32[512,3584]{1,0:T(8,128)} fusion(bf16[1,3584,512]{2,1,0:T(8,128)(2,1)} %param.11, f32[512,512]{1,0:T(8,128)S(1)} %fusion.12, bf16[512,3584]{1,0:T(8,128)(2,1)} %reshape.68, bf16[1,3584,512]{2,1,0:T(8,128)(2,1)} %param.12, f32[512,512]{1,0:T(8,128)S(1)} %fusion.4), kind=kOutput, calls=%fused_computation.6 | convolution fusion | flops 3760717824 | bytes 20447232 | tf_op jit(solution)/shard_map/dot_general | solution.py:27
  371.4 8.2 %add_convert_fusion = bf16[512,3584]{1,0:T(8,128)(2,1)} fusion(f32[512,3584]{1,0:T(8,128)} %fusion.2, bf16[1,3584,512]{2,1,0:T(8,128)(2,1)} %param.12, f32[512,512]{1,0:T(8,128)S(1)} %fusion.12, f32[512,512]{1,0:T(8,128)S(1)} %fusion.4), kind=kOutput, calls=%fused_computation.1 | convolution fusion | flops 1884291072 | bytes 16777216 | tf_op jit(solution)/shard_map/dot_general | solution.py:28
  379.7 8.1 %reshape.69 = bf16[16,16,2,3584]{3,2,1,0:T(2,128)(2,1)} reshape(bf16[512,3584]{1,0:T(8,128)(2,1)} %add_convert_fusion) | data formatting | bytes 7340032 | tf_op jit(solution)/shard_map/reshape | solution.py:31
  387.8 5.4 copy.89
  393.2 90.2 %all_to_all.41 = bf16[16,16,2,3584]{3,2,0,1:T(2,128)(2,1)S(1)} all-to-all(bf16[16,16,2,3584]{3,2,0,1:T(2,128)(2,1)S(1)} %copy.89), channel_id=1, replica_groups=mesh['node'=16,'local'=16] {'local'}, dimensions={1} | all-to-all | bytes 7340032 | tf_op jit(solution)/shard_map/all_to_all | solution.py:77
  483.4 3.8 copy.90
  487.3 4.5 all-to-all-start.7
  492.0 55.5 %all-to-all-done.7 = bf16[16,16,2,3584]{3,1,2,0:T(8,128)(2,1)} async-done(((bf16[16,16,2,3584]{3,1,2,0:T(8,128)(2,1)}), bf16[16,16,2,3584]{3,1,2,0:T(8,128)(2,1)}, u32[]{:S(2)}, u32[]{:S(2)}) %all-to-all-start.7) | async-done | bytes 3670048 | tf_op jit(solution)/shard_map/all_to_all | solution.py:78
  547.6 5.0 fusion.11
  (30 shorter events, 4.8 us)
Async XLA Ops:
  0.0 27.1 %copy-start = (bf16[64,3584]{1,0:T(8,128)(2,1)S(1)}, bf16[64,3584]{1,0:T(8,128)(2,1)}, u32[]{:S(2)}) copy-start(bf16[64,3584]{1,0:T(8,128)(2,1)} %param.8) | copy-start | bytes 1376260
  16.5 17.5 %all-to-all-start.1 = ((bf16[16,16,2]{0,2,1:T(2,128)(2,1)}), bf16[16,16,2]{0,2,1:T(2,128)(2,1)S(1)}, u32[]{:S(2)}, u32[]{:S(2)}) async-start(bf16[16,16,2]{0,2,1:T(2,128)(2,1)} %copy.80), calls=%async_computation.1 | async-start | bytes 16384 | tf_op jit(solution)/shard_map/all_to_all | solution.py:74
  38.0 4.6 copy-start.3
  38.0 59.9 %all-to-all-start.2 = ((bf16[16,16,2,3584]{3,2,1,0:T(2,128)(2,1)}), bf16[16,16,2,3584]{3,2,1,0:T(2,128)(2,1)}, u32[]{:S(2)}, u32[]{:S(2)}) async-start(bf16[16,16,2,3584]{3,2,1,0:T(2,128)(2,1)} %bitcast.56), calls=%async_computation.2 | async-start | bytes 7340032 | tf_op jit(solution)/shard_map/all_to_all | solution.py:68
  102.0 57.3 %all-to-all-start.4 = ((bf16[16,16,2,3584]{3,2,1,0:T(2,128)(2,1)}), bf16[16,16,2,3584]{3,2,1,0:T(2,128)(2,1)}, u32[]{:S(2)}, u32[]{:S(2)}) async-start(bf16[16,16,2,3584]{3,2,1,0:T(2,128)(2,1)} %bitcast.57), calls=%async_computation.4 | async-start | bytes 7340032 | tf_op jit(solution)/shard_map/all_to_all | solution.py:67
  159.3 89.3 %all-to-all-start.3 = ((bf16[16,16,2,3584]{3,2,0,1:T(2,128)(2,1)}), bf16[16,16,2,3584]{3,2,0,1:T(2,128)(2,1)}, u32[]{:S(2)}, u32[]{:S(2)}) async-start(bf16[16,16,2,3584]{3,2,0,1:T(2,128)(2,1)} %copy.84), calls=%async_computation.3 | async-start | bytes 7340032 | tf_op jit(solution)/shard_map/all_to_all | solution.py:73
  248.5 88.4 %all-to-all-start.5 = ((bf16[16,16,2,3584]{3,2,0,1:T(2,128)(2,1)}), bf16[16,16,2,3584]{3,2,0,1:T(2,128)(2,1)}, u32[]{:S(2)}, u32[]{:S(2)}) async-start(bf16[16,16,2,3584]{3,2,0,1:T(2,128)(2,1)} %copy.87), calls=%async_computation.5 | async-start | bytes 7340032 | tf_op jit(solution)/shard_map/all_to_all | solution.py:72
  352.6 5.4 copy-start.2
  352.6 5.4 copy-start.4
  487.3 60.2 %all-to-all-start.7 = ((bf16[16,16,2,3584]{3,1,2,0:T(8,128)(2,1)}), bf16[16,16,2,3584]{3,1,2,0:T(8,128)(2,1)}, u32[]{:S(2)}, u32[]{:S(2)}) async-start(bf16[16,16,2,3584]{3,1,2,0:T(8,128)(2,1)} %copy.90), calls=%async_computation.7 | async-start | bytes 7340032 | tf_op jit(solution)/shard_map/all_to_all | solution.py:78
  491.8 60.8 %copy-start.1 = (bf16[64,3584]{1,0:T(8,128)(2,1)S(1)}, bf16[64,3584]{1,0:T(8,128)(2,1)}, u32[]{:S(2)}) copy-start(bf16[64,3584]{1,0:T(8,128)(2,1)} %param.8) | copy-start | bytes 1376260
where the time goes:
time: 561 us; the launch traced here: 553 us
  waiting for transfers between devices  299 us (53%)
  blocking collectives  104 us (19%)
  local copies, waits for them, and re-layouts  76.8 us (14%)
  starting transfers between devices  37.5 us (7%)
  matrix products  33.3 us (6%)
    all_to_all x1, blocking collectives, shards(): lax.all_to_all(partials, 'local', split_axis=1, concat_axis=1, tiled=True)  90.2 us
    all_to_all x1, waiting for transfers between devices, shards(): lax.all_to_all(grad_slots, 'local', split_axis=1, concat_axis=1, tiled=True)  75.2 us
    all_to_all x1, waiting for transfers between devices, shards(): lax.all_to_all(x_slots, 'local', split_axis=1, concat_axis=1, tiled=True)  66.1 us
    all_to_all x1, waiting for transfers between devices, shards(): lax.all_to_all(returned, 'node', split_axis=0, concat_axis=0, tiled=True)  55.5 us
    all_to_all x1, waiting for transfers between devices, shards(): lax.all_to_all(grad_slots, 'node', split_axis=0, concat_axis=0, tiled=True)  52.7 us
    all_to_all x1, waiting for transfers between devices, shards(): lax.all_to_all(x_slots, 'node', split_axis=0, concat_axis=0, tiled=True)  45.1 us
    all_to_all x1, blocking collectives, shards(): lax.all_to_all(gate_slot, 'node', split_axis=0, concat_axis=0, tiled=True)  13.8 us
    reshape x2, local copies, waits for them, and re-layouts, expert_rows(): return result.astype(jnp.bfloat16).reshape(layout)  13.5 us
  transfers between devices with their start and end apart: 6, of which 6 were waited for; matrix products, arithmetic and copies ran while one was open for 7% of the time, Pallas kernels for 0%

commit v1 on v0

v1 whole, which is shorter than its diff:
```python
import functools

import jax
import jax.numpy as jnp
from jax import lax
from jax.experimental import pallas as pl
from jax.experimental.pallas import tpu as pltpu
from jax.sharding import PartitionSpec as P

SLOTS = 2
CHUNK = 512
AHEAD = 2
MESH = pl.DeviceIdType.MESH
LAST = (((1,), (1,)), ((), ()))
F32 = jnp.float32
BF16 = jnp.bfloat16


def iota(shape, dim):
    return lax.broadcasted_iota(jnp.int32, shape, dim)


def kernel(
    nodes, zs, chunks, width,
    x_ref, g_ref, exp_ref, gate_ref, wg_hbm, wu_hbm, wd_hbm, out_ref,
    pick, combine, sort_in, sort_out, wg, wu, wd, acc_a, acc_b, acc_d, da, db,
    z_send, z_recv, n_send, n_recv, own, half_send, half_recv,
    back_send, back_recv, home_send, home_recv,
    w_sem, send_sem, recv_sem, local_sem,
):
    node = lax.axis_index("node")
    local = lax.axis_index("local")
    z = local // 2
    core = local % 2
    sibling = z * 2 + (1 - core)
    toks = x_ref.shape[0]
    per_z = nodes * SLOTS
    per_n = zs * SLOTS
    slots = nodes * zs * SLOTS

    weights = [
        pltpu.make_async_copy(src.at[0], dst, w_sem.at[i])
        for i, (src, dst) in enumerate(((wg_hbm, wg), (wu_hbm, wu), (wd_hbm, wd)))
    ]
    for copy in weights:
        copy.start()

    barrier = pltpu.get_barrier_semaphore()
    for j in range(1, zs):
        pl.semaphore_signal(
            barrier, inc=1, device_id=(node, lax.rem(z + j, zs) * 2 + core), device_id_type=MESH
        )
    for j in range(1, nodes):
        pl.semaphore_signal(
            barrier, inc=1, device_id=(lax.rem(node + j, nodes), local), device_id_type=MESH
        )
    pl.semaphore_signal(barrier, inc=1, device_id=(node, sibling), device_id_type=MESH)

    slot = iota((slots, toks), 0)
    expert = (slot % per_z) // SLOTS * zs + slot // per_z
    first = exp_ref[0:1, :] == expert
    second = exp_ref[1:2, :] == expert
    hit = (first | second).astype(F32)
    earlier = (iota((toks, toks), 0) < iota((toks, toks), 1)).astype(BF16)
    rank = jnp.dot(hit.astype(BF16), earlier, preferred_element_type=F32)
    chosen = jnp.where(rank == (slot % SLOTS).astype(F32), hit, 0.0)
    pick[...] = chosen.astype(BF16)
    gates = jnp.where(first, gate_ref[0:1, :].astype(F32), gate_ref[1:2, :].astype(F32))
    weighted = (chosen * gates).astype(BF16)
    eye = (iota((toks, toks), 0) == iota((toks, toks), 1)).astype(BF16)
    combine[...] = lax.dot_general(eye, weighted, LAST, preferred_element_type=F32).astype(BF16)
    row = iota((slots, slots), 0)
    col = iota((slots, slots), 1)
    wanted = (row % per_n) // SLOTS * per_z + row // per_n * SLOTS + row % SLOTS
    sort_in[...] = (col == wanted).astype(F32).astype(BF16)
    wanted = (row % per_z) // SLOTS * per_n + row // per_z * SLOTS + row % SLOTS
    sort_out[...] = (col == wanted).astype(F32).astype(BF16)
    acc_a[...] = jnp.zeros_like(acc_a)
    acc_b[...] = jnp.zeros_like(acc_b)
    acc_d[...] = jnp.zeros_like(acc_d)

    def columns(k):
        return pl.ds(pl.multiple_of(k * width, width), width)

    def remote(phase, k, src, dst, device):
        return pltpu.make_async_remote_copy(
            src_ref=src, dst_ref=dst, send_sem=send_sem.at[phase, k],
            recv_sem=recv_sem.at[phase, k], device_id=device, device_id_type=MESH,
        )

    def spread(phase, k, src, dst, along_z):
        here, count = (z, zs) if along_z else (node, nodes)
        pltpu.make_async_copy(src.at[here], dst.at[here], local_sem.at[phase, k]).start()
        for j in range(1, count):
            to = lax.rem(here + j, count)
            device = (node, to * 2 + core) if along_z else (to, local)
            remote(phase, k, src.at[to], dst.at[here], device).start()

    def arrive(phase, k, src, dst, along_z):
        here, count = (z, zs) if along_z else (node, nodes)
        pltpu.make_async_copy(src.at[here], dst.at[here], local_sem.at[phase, k]).wait()
        rest = pl.ds(0, count - 1)
        remote(phase, k, src.at[rest], dst.at[rest], (node, sibling)).wait_recv()

    def leave(phase, k, src, count):
        rest = pl.ds(0, count - 1)
        remote(phase, k, src.at[rest], src.at[rest], (node, sibling)).wait_send()

    def select(k):
        for part, ref in enumerate((x_ref, g_ref)):
            rows = jnp.dot(pick[...], ref[:, columns(k)], preferred_element_type=F32)
            z_send[k, :, part * per_z:(part + 1) * per_z, :] = rows.astype(BF16).reshape(
                zs, per_z, width
            )
        spread(0, k, z_send.at[k], z_recv.at[k], True)

    def resort(k):
        arrive(0, k, z_send.at[k], z_recv.at[k], True)
        for part in range(2):
            rows = z_recv[k, :, part * per_z:(part + 1) * per_z, :].reshape(slots, width)
            rows = jnp.dot(sort_in[...], rows, preferred_element_type=F32)
            n_send[k, :, part * per_n:(part + 1) * per_n, :] = rows.astype(BF16).reshape(
                nodes, per_n, width
            )
        spread(1, k, n_send.at[k], n_recv.at[k, 0], False)

    def share(k):
        arrive(1, k, n_send.at[k], n_recv.at[k, 0], False)
        remote(2, k, n_recv.at[k, 0], n_recv.at[k, 1], (node, sibling)).start()

    def multiply(k):
        remote(2, k, n_recv.at[k, 0], n_recv.at[k, 1], (node, sibling)).wait_recv()
        rows = n_recv[k, :, :, 0:per_n, :].reshape(2 * slots, width)
        acc_a[...] += jnp.dot(rows, wg[columns(k), :], preferred_element_type=F32)
        acc_b[...] += jnp.dot(rows, wu[columns(k), :], preferred_element_type=F32)
        rows = n_recv[k, :, :, per_n:2 * per_n, :].reshape(2 * slots, width)
        acc_d[...] += lax.dot_general(rows, wd[:, columns(k)], LAST, preferred_element_type=F32)

    def project(k):
        part = lax.dot_general(da[...], wg[columns(k), :], LAST, preferred_element_type=F32)
        part += lax.dot_general(db[...], wu[columns(k), :], LAST, preferred_element_type=F32)
        own[k] = part[0:slots]
        half_send[k] = part[slots:2 * slots].astype(BF16)
        remote(3, k, half_send.at[k], half_recv.at[k], (node, sibling)).start()

    def add_halves(k):
        remote(3, k, half_send.at[k], half_recv.at[k], (node, sibling)).wait_recv()
        rows = (own[k] + half_recv[k].astype(F32)).astype(BF16)
        back_send[k] = rows.reshape(nodes, per_n, width)
        spread(4, k, back_send.at[k], back_recv.at[k], False)

    def unsort(k):
        arrive(4, k, back_send.at[k], back_recv.at[k], False)
        rows = back_recv[k].reshape(slots, width)
        rows = jnp.dot(sort_out[...], rows, preferred_element_type=F32)
        home_send[k] = rows.astype(BF16).reshape(zs, per_z, width)
        spread(5, k, home_send.at[k], home_recv.at[k], True)

    def gather(k):
        arrive(5, k, home_send.at[k], home_recv.at[k], True)
        rows = home_recv[k].reshape(slots, width)
        out_ref[:, columns(k)] = jnp.dot(
            combine[...], rows, preferred_element_type=F32
        ).astype(BF16)

    def when(i, lag, stage):
        @pl.when((i >= lag) & (i < chunks + lag))
        def _():
            stage(i - lag)

    pl.semaphore_wait(barrier, zs + nodes - 1)

    def dispatch(i, carry):
        when(i, 0, select)
        when(i, AHEAD, resort)
        when(i, AHEAD + 1, share)

        @pl.when(i == AHEAD + 2)
        def _():
            for copy in weights:
                copy.wait()

        when(i, AHEAD + 2, multiply)
        return carry

    lax.fori_loop(0, chunks + AHEAD + 2, dispatch, 0)

    a = acc_a[...]
    sig = jax.nn.sigmoid(a)
    grad = acc_d[...] * sig
    da[...] = (grad * acc_b[...] * (1.0 + a * (1.0 - sig))).astype(BF16)
    db[...] = (grad * a).astype(BF16)

    def combine_step(i, carry):
        when(i, 0, project)
        when(i, 1, add_halves)
        when(i, 2, unsort)
        when(i, 4, gather)
        return carry

    lax.fori_loop(0, chunks + 4, combine_step, 0)

    def drain(k, carry):
        leave(0, k, z_send.at[k], zs)
        leave(1, k, n_send.at[k], nodes)
        remote(2, k, n_recv.at[k, 0], n_recv.at[k, 1], (node, sibling)).wait_send()
        remote(3, k, half_send.at[k], half_recv.at[k], (node, sibling)).wait_send()
        leave(4, k, back_send.at[k], nodes)
        leave(5, k, home_send.at[k], zs)
        return carry

    lax.fori_loop(0, chunks, drain, 0)


def shards(inputs, out_grad, experts, gate_values, gate_matrix, up_matrix, down_matrix):
    nodes = lax.axis_size("node")
    zs = lax.axis_size("local") // 2
    toks, model = inputs.shape
    hidden = gate_matrix.shape[2]
    width = CHUNK
    chunks = model // width
    per_z = nodes * SLOTS
    per_n = zs * SLOTS
    slots = nodes * zs * SLOTS
    vmem = pl.BlockSpec(memory_space=pltpu.VMEM)
    hbm = pl.BlockSpec(memory_space=pl.ANY)
    return pl.pallas_call(
        functools.partial(kernel, nodes, zs, chunks, width),
        out_shape=jax.ShapeDtypeStruct((toks, model), BF16),
        in_specs=[vmem] * 4 + [hbm] * 3,
        out_specs=vmem,
        scratch_shapes=[
            pltpu.VMEM((slots, toks), BF16),
            pltpu.VMEM((toks, slots), BF16),
            pltpu.VMEM((slots, slots), BF16),
            pltpu.VMEM((slots, slots), BF16),
            pltpu.VMEM((model, hidden), BF16),
            pltpu.VMEM((model, hidden), BF16),
            pltpu.VMEM((hidden, model), BF16),
            pltpu.VMEM((2 * slots, hidden), F32),
            pltpu.VMEM((2 * slots, hidden), F32),
            pltpu.VMEM((2 * slots, hidden), F32),
            pltpu.VMEM((2 * slots, hidden), BF16),
            pltpu.VMEM((2 * slots, hidden), BF16),
            pltpu.VMEM((chunks, zs, 2 * per_z, width), BF16),
            pltpu.VMEM((chunks, zs, 2 * per_z, width), BF16),
            pltpu.VMEM((chunks, nodes, 2 * per_n, width), BF16),
            pltpu.VMEM((chunks, 2, nodes, 2 * per_n, width), BF16),
            pltpu.VMEM((chunks, slots, width), F32),
            pltpu.VMEM((chunks, slots, width), BF16),
            pltpu.VMEM((chunks, slots, width), BF16),
            pltpu.VMEM((chunks, nodes, per_n, width), BF16),
            pltpu.VMEM((chunks, nodes, per_n, width), BF16),
            pltpu.VMEM((chunks, zs, per_z, width), BF16),
            pltpu.VMEM((chunks, zs, per_z, width), BF16),
            pltpu.SemaphoreType.DMA((3,)),
            pltpu.SemaphoreType.DMA((6, chunks)),
            pltpu.SemaphoreType.DMA((6, chunks)),
            pltpu.SemaphoreType.DMA((6, chunks)),
        ],
        compiler_params=pltpu.CompilerParams(
            collective_id=0, has_side_effects=True, vmem_limit_bytes=60 * 1024 * 1024
        ),
        name="experts_backward",
    )(
        inputs, out_grad, experts.T, gate_values.T, gate_matrix, up_matrix, down_matrix
    )


def solution(mesh):
    rows = P(("node", "local"), None)
    stack = P(("node", "local"), None, None)
    return jax.shard_map(
        shards, mesh=mesh, in_specs=(rows,) * 4 + (stack,) * 3, out_specs=rows, check_vma=False
    )
```

time: 561 us -> 157 us (0.28)
  waiting for transfers between devices: 299 us -> 0 us
  Pallas kernels: 0 us -> 152 us
  blocking collectives: 104 us -> 0 us
  local copies, waits for them, and re-layouts: 76.8 us -> 1.82 us
  starting transfers between devices: 37.5 us -> 0 us
  matrix products: 33.3 us -> 0 us
    all_to_all x6 -> x0, waiting for transfers between devices: 299 us -> none  [the longest x1 75.2 us: shards(): lax.all_to_all(grad_slots, 'local', split_axis=1, concat_axis=1, tiled=True)]
    pallas_call x0 -> x1, Pallas kernels: none -> 152 us  [shards(): pl.pallas_call(functools.partial(kernel, nodes, zs, chunks, width), out_s...]
    all_to_all x2 -> x0, blocking collectives: 104 us -> none  [the longest x1 90.2 us: shards(): lax.all_to_all(partials, 'local', split_axis=1, concat_axis=1, tiled=True)]
    all_to_all x6 -> x0, starting transfers between devices: 37.5 us -> none  [the longest x1 10.6 us: shards(): lax.all_to_all(gate_slot, 'local', split_axis=1, concat_axis=1, tiled=True)]
    reshape x9 -> x0, local copies, waits for them, and re-layouts: 34.5 us -> none  [the longest x2 13.5 us: expert_rows(): return result.astype(jnp.bfloat16).reshape(layout)]
    all_to_all x7 -> x0, local copies, waits for them, and re-layouts: 33.7 us -> none  [the longest x1 7.32 us: shards(): lax.all_to_all(grad_slots, 'local', split_axis=1, concat_axis=1, tiled=True)]
    dot_general x7 -> x0, matrix products: 33.3 us -> none  [the longest x1 11.3 us: expert_rows(): lax.dot_general(grad_gate, w_gate, contract_last, preferred_element_type=...]
    broadcast_in_dim x4 -> x0, local copies, waits for them, and re-layouts: 8.13 us -> none  [the longest x1 4.06 us: shards(): jnp.repeat(x_slots.reshape(node_count, per_node, slot_cap, model_width),...]
  transfers between devices with their start and end apart: 6 -> 0, of which waited for: 6 -> 0; matrix products, arithmetic and copies ran while one was open for 7% -> 0% of each run, Pallas kernels for 0% -> 0%
where the time goes in v1:
time: 157 us; the launch traced here: 154 us
  Pallas kernels  152 us (97%)
  local copies, waits for them, and re-layouts  1.82 us (1%)
    pallas_call x1, Pallas kernels, shards(): pl.pallas_call(functools.partial(kernel, nodes, zs, chunks, width), out_s...  152 us

profile of v1, /device:TPU:1, one launch (start us, length us, event | category | flops | bytes accessed | tf_op | source)
XLA Modules:
  0.0 153.9 jit_solution(5903212636104991389)
XLA Ops:
  0.0 152.1 %experts_backward.1 = bf16[64,3584]{1,0:T(8,128)(2,1)} custom-call(bf16[64,3584]{1,0:T(8,128)(2,1)} %x_ref.1, bf16[64,3584]{1,0:T(8,128)(2,1)} %g_ref.1, s32[2,64]{1,0:T(2,128)} %bitcast.2, bf16[2,64]{1,0:T(2,128)(2,1)} %bitcast.3, bf16[1,3584,512]{2,1,0:T(8,128)(2,1)} %wg_hbm.1, bf16[1,3584,512]{2,1,0:T(8,128)(2,1)} %wu_hbm.1, bf16[1,512,3584]{2,1,0:T(8,128)(2,1)} %wd_hbm.1), custom_call_target="tpu_custom_call" | custom-call | tf_op jit(solution)/shard_map/experts_backward/pallas_call | solution.py:227
  152.1 1.8 %copy.9 = bf16[64,3584]{1,0:T(8,128)(2,1)} copy(bf16[64,3584]{1,0:T(8,128)(2,1)} %experts_backward.1) | data formatting | bytes 917504

commit v2 on v1

v2 whole, which is shorter than its diff:
```python
import functools

import jax
import jax.numpy as jnp
from jax import lax
from jax.experimental import pallas as pl
from jax.experimental.pallas import tpu as pltpu
from jax.sharding import PartitionSpec as P

SLOTS = 2
CAP = 24
CHUNK = 512
BACK_CHUNK = 512
AHEAD = 2
MESH = pl.DeviceIdType.MESH
LAST = (((1,), (1,)), ((), ()))
F32 = jnp.float32
BF16 = jnp.bfloat16


def iota(shape, dim):
    return lax.broadcasted_iota(jnp.int32, shape, dim)


def eye(n):
    return (iota((n, n), 0) == iota((n, n), 1)).astype(BF16)


def kernel(
    nodes, zs, cap, chunks, width, back_chunks, back_width,
    x_ref, g_ref, exp_ref, gate_ref, wg_hbm, wu_hbm, wd_hbm, out_ref, flag_ref,
    pick_x, pick_g, comb_lo, comb_hi, sort_x, sort_g, list_lo, list_hi,
    wg, wu, wd, acc_a, acc_b, acc_d, da, db,
    z_send, z_recv, n_send, n_recv, own, half_send, half_recv,
    back_send, back_recv, home_send, home_recv,
    meta_send, meta_recv, flag_n_send, flag_n_recv, flag_s_send, flag_s_recv,
    w_sem, send_sem, recv_sem, local_sem,
):
    node = lax.axis_index("node")
    local = lax.axis_index("local")
    z = local // 2
    core = local % 2
    sibling = (node, z * 2 + (1 - core))
    toks = x_ref.shape[0]
    per_n = zs * SLOTS
    slots = nodes * zs * SLOTS
    block = 2 * cap
    listed = zs * block

    weights = [
        pltpu.make_async_copy(src.at[0], dst, w_sem.at[i])
        for i, (src, dst) in enumerate(((wg_hbm, wg), (wu_hbm, wu), (wd_hbm, wd)))
    ]
    for copy in weights:
        copy.start()

    barrier = pltpu.get_barrier_semaphore()
    for j in range(1, zs):
        pl.semaphore_signal(
            barrier, inc=1, device_id=(node, lax.rem(z + j, zs) * 2 + core), device_id_type=MESH
        )
    for j in range(1, nodes):
        pl.semaphore_signal(
            barrier, inc=1, device_id=(lax.rem(node + j, nodes), local), device_id_type=MESH
        )
    pl.semaphore_signal(barrier, inc=1, device_id=sibling, device_id_type=MESH)

    earlier = (iota((toks, toks), 0) < iota((toks, toks), 1)).astype(BF16)

    def before(mask):
        return jnp.dot(mask.astype(BF16), earlier, preferred_element_type=F32)

    first = exp_ref[0:1, :]
    second = exp_ref[1:2, :]
    target = iota((listed, toks), 0) // block
    half = (iota((listed, toks), 0) % block) // cap
    place = (iota((listed, toks), 0) % cap).astype(F32)
    by_first = lax.rem(first, zs) == target
    by_second = lax.rem(second, zs) == target
    on_list = (by_first | by_second).astype(F32)
    chosen = jnp.where(before(on_list) == place, on_list, 0.0)
    pick_x[...] = jnp.where(half == 0, chosen, 0.0).astype(BF16)
    pick_g[...] = jnp.where(half == 1, chosen, 0.0).astype(BF16)
    gates = jnp.where(by_first, gate_ref[0:1, :].astype(F32), gate_ref[1:2, :].astype(F32))
    weighted = chosen * gates
    turn = eye(toks)
    for h, ref in enumerate((comb_lo, comb_hi)):
        ref[...] = lax.dot_general(
            turn, jnp.where(half == h, weighted, 0.0).astype(BF16), LAST,
            preferred_element_type=F32,
        ).astype(BF16)
    longest = jnp.max(jnp.sum(on_list, axis=1, keepdims=True), axis=0, keepdims=True)
    over = (longest > cap).astype(F32).astype(jnp.int32)
    meta_send[...] = jnp.zeros_like(meta_send) + over
    meta_send[0:1, 0:toks] = first
    meta_send[1:2, 0:toks] = second
    acc_a[...] = jnp.zeros_like(acc_a)
    acc_b[...] = jnp.zeros_like(acc_b)
    acc_d[...] = jnp.zeros_like(acc_d)

    def columns(k, size):
        return pl.ds(pl.multiple_of(k * size, size), size)

    def remote(phase, k, src, dst, device):
        return pltpu.make_async_remote_copy(
            src_ref=src, dst_ref=dst, send_sem=send_sem.at[phase, k],
            recv_sem=recv_sem.at[phase, k], device_id=device, device_id_type=MESH,
        )

    def spread(phase, k, src, dst, along_z, shared=False):
        here, count = (z, zs) if along_z else (node, nodes)
        mine = src if shared else src.at[here]
        pltpu.make_async_copy(mine, dst.at[here], local_sem.at[phase, k]).start()
        for j in range(1, count):
            to = lax.rem(here + j, count)
            device = (node, to * 2 + core) if along_z else (to, local)
            remote(phase, k, src if shared else src.at[to], dst.at[here], device).start()

    def arrive(phase, k, dst, along_z):
        here, count = (z, zs) if along_z else (node, nodes)
        pltpu.make_async_copy(dst.at[here], dst.at[here], local_sem.at[phase, k]).wait()
        rest = pl.ds(0, count - 1)
        remote(phase, k, dst.at[rest], dst.at[rest], sibling).wait_recv()

    def leave(phase, k, dst, count):
        rest = pl.ds(0, count - 1)
        remote(phase, k, dst.at[rest], dst.at[rest], sibling).wait_send()

    def select(k):
        rows = jnp.dot(pick_x[...], x_ref[:, columns(k, width)], preferred_element_type=F32)
        rows += jnp.dot(pick_g[...], g_ref[:, columns(k, width)], preferred_element_type=F32)
        z_send[k] = rows.astype(BF16).reshape(zs, block, width)
        spread(0, k, z_send.at[k], z_recv.at[k], True)

    def resort(k):
        arrive(0, k, z_recv.at[k], True)
        rows = z_recv[k].reshape(listed, width)
        for h, ref in enumerate((sort_x, sort_g)):
            part = jnp.dot(ref[...], rows, preferred_element_type=F32)
            n_send[k, :, h * per_n:(h + 1) * per_n, :] = part.astype(BF16).reshape(
                nodes, per_n, width
            )
        spread(1, k, n_send.at[k], n_recv.at[k, 0], False)

    def share(k):
        arrive(1, k, n_recv.at[k, 0], False)
        remote(2, k, n_recv.at[k, 0], n_recv.at[k, 1], sibling).start()

    def multiply(k):
        remote(2, k, n_recv.at[k, 0], n_recv.at[k, 1], sibling).wait_recv()
        rows = n_recv[k, :, :, 0:per_n, :].reshape(2 * slots, width)
        acc_a[...] += jnp.dot(rows, wg[columns(k, width), :], preferred_element_type=F32)
        acc_b[...] += jnp.dot(rows, wu[columns(k, width), :], preferred_element_type=F32)
        rows = n_recv[k, :, :, per_n:2 * per_n, :].reshape(2 * slots, width)
        acc_d[...] += lax.dot_general(
            rows, wd[:, columns(k, width)], LAST, preferred_element_type=F32
        )

    def project(k):
        cols = columns(k, back_width)
        part = lax.dot_general(da[...], wg[cols, :], LAST, preferred_element_type=F32)
        part += lax.dot_general(db[...], wu[cols, :], LAST, preferred_element_type=F32)
        own[k] = part[0:slots]
        half_send[k] = part[slots:2 * slots].astype(BF16)
        remote(3, k, half_send.at[k], half_recv.at[k], sibling).start()

    def add_halves(k):
        remote(3, k, half_send.at[k], half_recv.at[k], sibling).wait_recv()
        rows = (own[k] + half_recv[k].astype(F32)).astype(BF16)
        back_send[k] = rows.reshape(nodes, per_n, back_width)
        spread(4, k, back_send.at[k], back_recv.at[k], False)

    mid = back_width // 2

    def unsort(k):
        arrive(4, k, back_recv.at[k], False)
        rows = jnp.dot(
            list_lo[...], back_recv[k, :, :, 0:mid].reshape(slots, mid),
            preferred_element_type=F32,
        )
        rows += jnp.dot(
            list_hi[...], back_recv[k, :, :, mid:back_width].reshape(slots, mid),
            preferred_element_type=F32,
        )
        home_send[k] = rows.astype(BF16).reshape(zs, block, mid)
        spread(5, k, home_send.at[k], home_recv.at[k], True)

    def gather(k):
        arrive(5, k, home_recv.at[k], True)
        rows = home_recv[k].reshape(listed, mid)
        for h, ref in enumerate((comb_lo, comb_hi)):
            out_ref[:, pl.ds(pl.multiple_of(k * back_width + h * mid, mid), mid)] = jnp.dot(
                ref[...], rows, preferred_element_type=F32
            ).astype(BF16)

    def when(i, lag, count, stage):
        @pl.when((i >= lag) & (i < count + lag))
        def _():
            stage(i - lag)

    pl.semaphore_wait(barrier, zs + nodes - 1)
    spread(6, 0, meta_send, meta_recv, True, shared=True)
    for k in range(min(AHEAD, chunks)):
        select(k)

    arrive(6, 0, meta_recv, True)
    slot = iota((nodes * SLOTS, toks), 0)
    expert = slot // SLOTS * zs + z
    wanted = (slot % SLOTS).astype(F32)
    position = (iota((block, toks), 0) % cap).astype(F32)
    wide = iota((nodes * SLOTS, slots), 1)
    narrow = iota((nodes * SLOTS, slots), 0)
    same = (wide // per_n == narrow // SLOTS) & (wide % SLOTS == narrow % SLOTS)
    lower = iota((block, slots), 0) // cap
    flags = meta_recv[0]
    for q in range(zs):
        if q:
            flags = jnp.maximum(flags, meta_recv[q])
        first = meta_recv[q, 0:1, 0:toks]
        second = meta_recv[q, 1:2, 0:toks]
        names = ((first == expert) | (second == expert)).astype(F32)
        names = jnp.where(before(names) == wanted, names, 0.0)
        on_list = (lax.rem(first, zs) == z) | (lax.rem(second, zs) == z)
        on_list = jnp.broadcast_to(on_list.astype(F32), (block, toks))
        on_list = jnp.where(before(on_list) == position, on_list, 0.0)
        table = lax.dot_general(
            on_list.astype(BF16), names.astype(BF16), LAST, preferred_element_type=F32
        )
        place_q = (same & ((wide % per_n) // SLOTS == q)).astype(F32).astype(BF16)
        table = jnp.dot(table.astype(BF16), place_q, preferred_element_type=F32)
        list_lo[q * block:(q + 1) * block, :] = jnp.where(lower == 0, table, 0.0).astype(BF16)
        list_hi[q * block:(q + 1) * block, :] = jnp.where(lower == 1, table, 0.0).astype(BF16)
    turn = eye(slots)
    sort_x[...] = lax.dot_general(turn, list_lo[...], LAST, preferred_element_type=F32).astype(BF16)
    sort_g[...] = lax.dot_general(turn, list_hi[...], LAST, preferred_element_type=F32).astype(BF16)
    flag_n_send[...] = flags
    spread(7, 0, flag_n_send, flag_n_recv, False, shared=True)

    def dispatch(i, carry):
        @pl.when(i + AHEAD < chunks)
        def _():
            select(i + AHEAD)

        when(i, 0, chunks, resort)
        when(i, 1, chunks, share)

        @pl.when(i == 2)
        def _():
            for copy in weights:
                copy.wait()

        when(i, 2, chunks, multiply)
        return carry

    lax.fori_loop(0, chunks + 2, dispatch, 0)

    a = acc_a[...]
    sig = jax.nn.sigmoid(a)
    grad = acc_d[...] * sig
    da[...] = (grad * acc_b[...] * (1.0 + a * (1.0 - sig))).astype(BF16)
    db[...] = (grad * a).astype(BF16)

    def combine_step(i, carry):
        when(i, 0, back_chunks, project)
        when(i, 1, back_chunks, add_halves)
        when(i, 2, back_chunks, unsort)
        when(i, 4, back_chunks, gather)
        return carry

    lax.fori_loop(0, back_chunks + 4, combine_step, 0)

    arrive(7, 0, flag_n_recv, False)
    flags = flag_n_recv[0]
    for m in range(1, nodes):
        flags = jnp.maximum(flags, flag_n_recv[m])
    flag_s_send[...] = flags
    other = remote(8, 0, flag_s_send, flag_s_recv, sibling)
    other.start()
    other.wait_recv()
    flag_ref[...] = jnp.maximum(flags, flag_s_recv[...])

    def drain(k, carry):
        leave(0, k, z_recv.at[k], zs)
        leave(1, k, n_recv.at[k, 0], nodes)
        remote(2, k, n_recv.at[k, 0], n_recv.at[k, 1], sibling).wait_send()
        return carry

    lax.fori_loop(0, chunks, drain, 0)

    def drain_back(k, carry):
        remote(3, k, half_send.at[k], half_recv.at[k], sibling).wait_send()
        leave(4, k, back_recv.at[k], nodes)
        leave(5, k, home_recv.at[k], zs)
        return carry

    lax.fori_loop(0, back_chunks, drain_back, 0)
    leave(6, 0, meta_recv, zs)
    leave(7, 0, flag_n_recv, nodes)
    other.wait_send()


def exchange(cap, collective, inputs, out_grad, experts, gates, gate_matrix, up_matrix, down_matrix):
    nodes = lax.axis_size("node")
    zs = lax.axis_size("local") // 2
    toks, model = inputs.shape
    hidden = gate_matrix.shape[2]
    width, back_width = CHUNK, BACK_CHUNK
    chunks, back_chunks = model // width, model // back_width
    per_n = zs * SLOTS
    slots = nodes * zs * SLOTS
    block = 2 * cap
    listed = zs * block
    steps = max(chunks, back_chunks)
    vmem = pl.BlockSpec(memory_space=pltpu.VMEM)
    hbm = pl.BlockSpec(memory_space=pl.ANY)
    return pl.pallas_call(
        functools.partial(kernel, nodes, zs, cap, chunks, width, back_chunks, back_width),
        out_shape=(
            jax.ShapeDtypeStruct((toks, model), BF16),
            jax.ShapeDtypeStruct((8, 128), jnp.int32),
        ),
        in_specs=[vmem] * 4 + [hbm] * 3,
        out_specs=(vmem, vmem),
        scratch_shapes=[
            pltpu.VMEM((listed, toks), BF16),
            pltpu.VMEM((listed, toks), BF16),
            pltpu.VMEM((toks, listed), BF16),
            pltpu.VMEM((toks, listed), BF16),
            pltpu.VMEM((slots, listed), BF16),
            pltpu.VMEM((slots, listed), BF16),
            pltpu.VMEM((listed, slots), BF16),
            pltpu.VMEM((listed, slots), BF16),
            pltpu.VMEM((model, hidden), BF16),
            pltpu.VMEM((model, hidden), BF16),
            pltpu.VMEM((hidden, model), BF16),
            pltpu.VMEM((2 * slots, hidden), F32),
            pltpu.VMEM((2 * slots, hidden), F32),
            pltpu.VMEM((2 * slots, hidden), F32),
            pltpu.VMEM((2 * slots, hidden), BF16),
            pltpu.VMEM((2 * slots, hidden), BF16),
            pltpu.VMEM((chunks, zs, block, width), BF16),
            pltpu.VMEM((chunks, zs, block, width), BF16),
            pltpu.VMEM((chunks, nodes, 2 * per_n, width), BF16),
            pltpu.VMEM((chunks, 2, nodes, 2 * per_n, width), BF16),
            pltpu.VMEM((back_chunks, slots, back_width), F32),
            pltpu.VMEM((back_chunks, slots, back_width), BF16),
            pltpu.VMEM((back_chunks, slots, back_width), BF16),
            pltpu.VMEM((back_chunks, nodes, per_n, back_width), BF16),
            pltpu.VMEM((back_chunks, nodes, per_n, back_width), BF16),
            pltpu.VMEM((back_chunks, zs, block, back_width // 2), BF16),
            pltpu.VMEM((back_chunks, zs, block, back_width // 2), BF16),
            pltpu.VMEM((8, 128), jnp.int32),
            pltpu.VMEM((zs, 8, 128), jnp.int32),
            pltpu.VMEM((8, 128), jnp.int32),
            pltpu.VMEM((nodes, 8, 128), jnp.int32),
            pltpu.VMEM((8, 128), jnp.int32),
            pltpu.VMEM((8, 128), jnp.int32),
            pltpu.SemaphoreType.DMA((3,)),
            pltpu.SemaphoreType.DMA((9, steps)),
            pltpu.SemaphoreType.DMA((9, steps)),
            pltpu.SemaphoreType.DMA((9, steps)),
        ],
        compiler_params=pltpu.CompilerParams(
            collective_id=collective, has_side_effects=True, vmem_limit_bytes=60 * 1024 * 1024
        ),
        name=f"experts_backward_{cap}",
    )(inputs, out_grad, experts, gates, gate_matrix, up_matrix, down_matrix)


def shards(inputs, out_grad, experts, gate_values, gate_matrix, up_matrix, down_matrix):
    nodes = lax.axis_size("node")
    args = (inputs, out_grad, experts.T, gate_values.T, gate_matrix, up_matrix, down_matrix)
    result, flags = exchange(CAP, 0, *args)
    return lax.cond(
        flags[7, 127] > 0,
        lambda: exchange(nodes * SLOTS, 1, *args)[0],
        lambda: result,
    )


def solution(mesh):
    rows = P(("node", "local"), None)
    stack = P(("node", "local"), None, None)
    return jax.shard_map(
        shards, mesh=mesh, in_specs=(rows,) * 4 + (stack,) * 3, out_specs=rows, check_vma=False
    )
```

time: 157 us -> 133 us (0.85); the launches traced: 154 us -> 133 us
  Pallas kernels: 152 us -> 129 us
    pallas_call x1, Pallas kernels: 152 us -> 129 us  [exchange(): pl.pallas_call(functools.partial(kernel, nodes, zs, cap, chunks, width, b...]
where the time goes in v2:
time: 133 us
  Pallas kernels  129 us (97%)
  local copies, waits for them, and re-layouts  3.09 us (2%)
    pallas_call x1, Pallas kernels, exchange(): pl.pallas_call(functools.partial(kernel, nodes, zs, cap, chunks, width, b...  129 us

profile of v2, /device:TPU:1, one launch (start us, length us, event | category | flops | bytes accessed | tf_op | source)
XLA Modules:
  0.0 133.2 jit_solution(10735051303695542258)
XLA Ops:
  0.0 0.0 copy-start
  0.0 0.0 copy-start.1
  0.0 129.5 %experts_backward_24.1 = (bf16[64,3584]{1,0:T(8,128)(2,1)}, s32[8,128]{1,0:T(8,128)}) custom-call(bf16[64,3584]{1,0:T(8,128)(2,1)} %x_ref.1, bf16[64,3584]{1,0:T(8,128)(2,1)} %g_ref.1, s32[2,64]{1,0:T(2,128)} %bitcast.3, bf16[2,64]{1,0:T(2,128)(2,1)} %bitcast.5, bf16[1,3584,512]{2,1,0:T(8,128)(2,1)} %wg_hbm.1, bf16[1,3584,512]{2,1,0:T(8,128)(2,1)} %wu_hbm.1, ...), custom_call_target="tpu_custom_call" | custom-call | tf_op jit(solution)/shard_map/experts_backward_24/pallas_call | solution.py:316
  129.5 1.3 slice.3
  131.4 0.0 copy-done
  131.4 0.0 copy-done.1
  131.4 1.8 %copy.13 = bf16[64,3584]{1,0:T(8,128)(2,1)} copy(bf16[64,3584]{1,0:T(8,128)(2,1)} %get-tuple-element.35) | data formatting | bytes 917504
  (1 shorter events, 0.0 us)
Async XLA Ops:
  0.0 131.4 %copy-start = (bf16[1,3584,512]{2,1,0:T(8,128)(2,1)S(1)}, bf16[1,3584,512]{2,1,0:T(8,128)(2,1)}, u32[]{:S(2)}) copy-start(bf16[1,3584,512]{2,1,0:T(8,128)(2,1)} %wg_hbm.1) | copy-start | bytes 11010052
  0.0 131.4 %copy-start.1 = (bf16[64,3584]{1,0:T(8,128)(2,1)S(1)}, bf16[64,3584]{1,0:T(8,128)(2,1)}, u32[]{:S(2)}) copy-start(bf16[64,3584]{1,0:T(8,128)(2,1)} %x_ref.1) | copy-start | bytes 1376260

commit v3 on v0

--- a/solution.py
+++ b/solution.py
@@ -1,9 +1,413 @@
+import functools
+
 import jax
 import jax.numpy as jnp
 from jax import lax
+from jax.experimental import pallas as pl
+from jax.experimental.pallas import tpu as pltpu
 from jax.sharding import PartitionSpec as P
 
-NODES_TOK = 1
+SLOTS = 2
+CAP = 24
+OUT_SEGMENTS = ((5, 512), (2, 256), (4, 128))
+BACK_SEGMENTS = ((1, 256), (6, 512), (1, 256))
+AHEAD = 2
+MESH = pl.DeviceIdType.MESH
+LAST = (((1,), (1,)), ((), ()))
+F32 = jnp.float32
+BF16 = jnp.bfloat16
+
+
+def iota(shape, dim):
+    return lax.broadcasted_iota(jnp.int32, shape, dim)
+
+
+def eye(n):
+    return (iota((n, n), 0) == iota((n, n), 1)).astype(BF16)
+
+
+class Chunk:
+    def __init__(self, segment, k):
+        self.buffers, self.width, self.begin, self.first = segment
+        self.k = k
+        self.sem = self.first + k
+
+    def columns(self, part=0, parts=1):
+        size = self.width // parts
+        start = self.begin + self.k * self.width + part * size
+        return pl.ds(start if isinstance(start, int) else pl.multiple_of(start, 128), size)
+
+    def at(self, i, *rest):
+        return self.buffers[i].at[(self.k, *rest)]
+
+    def get(self, i):
+        return self.buffers[i][self.k]
+
+
+def split(segments, refs):
+    result, begin, first = [], 0, 0
+    each = len(refs) // len(segments)
+    for n, (count, width) in enumerate(segments):
+        result.append(((refs[n * each:(n + 1) * each], width, begin, first), count))
+        begin += count * width
+        first += count
+    return result, first
+
+
+def kernel(
+    nodes, zs, cap,
+    x_ref, g_ref, exp_ref, gate_ref, wg_hbm, wu_hbm, wd_hbm, out_ref, flag_ref,
+    pick_x, pick_g, comb_lo, comb_hi, sort_x, sort_g, list_lo, list_hi,
+    wg, wu, wd, acc_a, acc_b, acc_d, da, db,
+    meta_send, meta_recv, flag_n_send, flag_n_recv, flag_s_send, flag_s_recv,
+    w_sem, send_sem, recv_sem, local_sem, *rest,
+):
+    z_send, z_recv, n_send, n_recv = range(4)
+    own, half_send, half_recv, back_send, back_recv, home_send, home_recv = range(7)
+    out_segments, out_steps = split(OUT_SEGMENTS, rest[:4 * len(OUT_SEGMENTS)])
+    back_segments, back_steps = split(BACK_SEGMENTS, rest[4 * len(OUT_SEGMENTS):])
+    node = lax.axis_index("node")
+    local = lax.axis_index("local")
+    z = local // 2
+    core = local % 2
+    sibling = (node, z * 2 + (1 - core))
+    toks = x_ref.shape[0]
+    per_n = zs * SLOTS
+    slots = nodes * zs * SLOTS
+    block = 2 * cap
+    listed = zs * block
+
+    weights = [
+        pltpu.make_async_copy(src.at[0], dst, w_sem.at[i])
+        for i, (src, dst) in enumerate(((wg_hbm, wg), (wu_hbm, wu), (wd_hbm, wd)))
+    ]
+    for copy in weights:
+        copy.start()
+
+    barrier = pltpu.get_barrier_semaphore()
+    for j in range(1, zs):
+        pl.semaphore_signal(
+            barrier, inc=1, device_id=(node, lax.rem(z + j, zs) * 2 + core), device_id_type=MESH
+        )
+    for j in range(1, nodes):
+        pl.semaphore_signal(
+            barrier, inc=1, device_id=(lax.rem(node + j, nodes), local), device_id_type=MESH
+        )
+    pl.semaphore_signal(barrier, inc=1, device_id=sibling, device_id_type=MESH)
+
+    earlier = (iota((toks, toks), 0) < iota((toks, toks), 1)).astype(BF16)
+
+    def before(mask):
+        return jnp.dot(mask.astype(BF16), earlier, preferred_element_type=F32)
+
+    first = exp_ref[0:1, :]
+    second = exp_ref[1:2, :]
+    target = iota((zs, toks), 0)
+    by_first = lax.rem(first, zs) == target
+    by_second = lax.rem(second, zs) == target
+    on_list = (by_first | by_second).astype(F32)
+
+    def expand(rows):
+        return jnp.broadcast_to(rows[:, None, :], (zs, block, toks)).reshape(listed, toks)
+
+    order = iota((zs, block, toks), 1).reshape(listed, toks)
+    upper = order >= cap
+    place = jnp.where(upper, order - cap, order).astype(F32)
+    chosen = jnp.where(expand(before(on_list)) == place, expand(on_list), 0.0)
+    pick_x[...] = jnp.where(upper, 0.0, chosen).astype(BF16)
+    pick_g[...] = jnp.where(upper, chosen, 0.0).astype(BF16)
+    longest = jnp.max(jnp.sum(on_list, axis=1, keepdims=True), axis=0, keepdims=True)
+    over = (longest > cap).astype(F32).astype(jnp.int32)
+    meta_send[...] = jnp.zeros_like(meta_send) + over
+    meta_send[0:1, 0:toks] = first
+    meta_send[1:2, 0:toks] = second
+
+    def remote(phase, k, src, dst, device):
+        return pltpu.make_async_remote_copy(
+            src_ref=src, dst_ref=dst, send_sem=send_sem.at[phase, k],
+            recv_sem=recv_sem.at[phase, k], device_id=device, device_id_type=MESH,
+        )
+
+    def spread(phase, k, src, dst, along_z, shared=False):
+        here, count = (z, zs) if along_z else (node, nodes)
+        mine = src if shared else src.at[here]
+        pltpu.make_async_copy(mine, dst.at[here], local_sem.at[phase, k]).start()
+        for j in range(1, count):
+            to = lax.rem(here + j, count)
+            device = (node, to * 2 + core) if along_z else (to, local)
+            remote(phase, k, src if shared else src.at[to], dst.at[here], device).start()
+
+    def arrive(phase, k, dst, along_z):
+        here, count = (z, zs) if along_z else (node, nodes)
+        pltpu.make_async_copy(dst.at[here], dst.at[here], local_sem.at[phase, k]).wait()
+        rest = pl.ds(0, count - 1)
+        remote(phase, k, dst.at[rest], dst.at[rest], sibling).wait_recv()
+
+    def leave(phase, k, dst, count):
+        rest = pl.ds(0, count - 1)
+        remote(phase, k, dst.at[rest], dst.at[rest], sibling).wait_send()
+
+    def select(c):
+        rows = jnp.dot(pick_x[...], x_ref[:, c.columns()], preferred_element_type=F32)
+        rows += jnp.dot(pick_g[...], g_ref[:, c.columns()], preferred_element_type=F32)
+        c.buffers[z_send][c.k] = rows.astype(BF16).reshape(zs, block, c.width)
+        spread(0, c.sem, c.at(z_send), c.at(z_recv), True)
+
+    def resort(c):
+        arrive(0, c.sem, c.at(z_recv), True)
+        rows = c.get(z_recv).reshape(listed, c.width)
+        for h, ref in enumerate((sort_x, sort_g)):
+            part = jnp.dot(ref[...], rows, preferred_element_type=F32)
+            c.buffers[n_send][c.k, :, h * per_n:(h + 1) * per_n, :] = part.astype(BF16).reshape(
+                nodes, per_n, c.width
+            )
+        spread(1, c.sem, c.at(n_send), c.at(n_recv, 0), False)
+
+    def to_sibling(c):
+        return remote(2, c.sem, c.at(n_recv, 0), c.at(n_recv, 1), sibling)
+
+    def share(c):
+        arrive(1, c.sem, c.at(n_recv, 0), False)
+        to_sibling(c).start()
+
+    def multiply(c):
+        to_sibling(c).wait_recv()
+        cols = c.columns()
+        rows = c.buffers[n_recv][c.k, :, :, 0:per_n, :].reshape(2 * slots, c.width)
+        acc_a[...] += jnp.dot(rows, wg[cols, :], preferred_element_type=F32)
+        acc_b[...] += jnp.dot(rows, wu[cols, :], preferred_element_type=F32)
+        rows = c.buffers[n_recv][c.k, :, :, per_n:2 * per_n, :].reshape(2 * slots, c.width)
+        acc_d[...] += lax.dot_general(rows, wd[:, cols], LAST, preferred_element_type=F32)
+
+    def release(c):
+        leave(0, c.sem, c.at(z_recv), zs)
+        leave(1, c.sem, c.at(n_recv, 0), nodes)
+        to_sibling(c).wait_send()
+
+    def halves(c):
+        return remote(3, c.sem, c.at(half_send), c.at(half_recv), sibling)
+
+    def project(c):
+        cols = c.columns()
+        part = lax.dot_general(da[...], wg[cols, :], LAST, preferred_element_type=F32)
+        part += lax.dot_general(db[...], wu[cols, :], LAST, preferred_element_type=F32)
+        c.buffers[half_send][c.k] = part[slots:2 * slots].astype(BF16)
+        halves(c).start()
+        c.buffers[own][c.k] = part[0:slots]
+
+    def add_halves(c):
+        halves(c).wait_recv()
+        rows = (c.get(own) + c.get(half_recv).astype(F32)).astype(BF16)
+        c.buffers[back_send][c.k] = rows.reshape(nodes, per_n, c.width)
+        spread(4, c.sem, c.at(back_send), c.at(back_recv), False)
+
+    def unsort(c):
+        arrive(4, c.sem, c.at(back_recv), False)
+        mid = c.width // 2
+        rows = jnp.dot(
+            list_lo[...], c.buffers[back_recv][c.k, :, :, 0:mid].reshape(slots, mid),
+            preferred_element_type=F32,
+        )
+        rows += jnp.dot(
+            list_hi[...], c.buffers[back_recv][c.k, :, :, mid:c.width].reshape(slots, mid),
+            preferred_element_type=F32,
+        )
+        c.buffers[home_send][c.k] = rows.astype(BF16).reshape(zs, block, mid)
+        spread(5, c.sem, c.at(home_send), c.at(home_recv), True)
+
+    def gather(c):
+        halves(c).wait_send()
+        leave(4, c.sem, c.at(back_recv), nodes)
+        arrive(5, c.sem, c.at(home_recv), True)
+        rows = c.get(home_recv).reshape(listed, c.width // 2)
+        for h, ref in enumerate((comb_lo, comb_hi)):
+            out_ref[:, c.columns(h, 2)] = jnp.dot(
+                ref[...], rows, preferred_element_type=F32
+            ).astype(BF16)
+        leave(5, c.sem, c.at(home_recv), zs)
+
+    def when(i, lag, segments, stage):
+        for segment, count in segments:
+            start = segment[3] + lag
+
+            @pl.when((i >= start) & (i < start + count))
+            def _():
+                stage(Chunk(segment, i - start))
+
+    pl.semaphore_wait(barrier, zs + nodes - 1)
+    spread(6, 0, meta_send, meta_recv, True, shared=True)
+    early = [Chunk(segment, k) for segment, count in out_segments for k in range(count)][:AHEAD]
+    for c in early:
+        select(c)
+
+    gates = jnp.where(by_first, gate_ref[0:1, :].astype(F32), gate_ref[1:2, :].astype(F32))
+    weighted = chosen * expand(gates)
+    turn = eye(toks)
+    for ref, mask in ((comb_lo, ~upper), (comb_hi, upper)):
+        ref[...] = lax.dot_general(
+            turn, jnp.where(mask, weighted, 0.0).astype(BF16), LAST, preferred_element_type=F32
+        ).astype(BF16)
+    acc_a[...] = jnp.zeros_like(acc_a)
+    acc_b[...] = jnp.zeros_like(acc_b)
+    acc_d[...] = jnp.zeros_like(acc_d)
+
+    arrive(6, 0, meta_recv, True)
+    slot = iota((nodes * SLOTS, toks), 0)
+    expert = slot // SLOTS * zs + z
+    wanted = (slot % SLOTS).astype(F32)
+    position = order[0:block]
+    position = jnp.where(position >= cap, position - cap, position).astype(F32)
+    wide = iota((nodes * SLOTS, slots), 1)
+    narrow = iota((nodes * SLOTS, slots), 0)
+    same = (wide // per_n == narrow // SLOTS) & (wide % SLOTS == narrow % SLOTS)
+    lower = iota((block, slots), 0) < cap
+    flags = meta_recv[0]
+    for q in range(zs):
+        if q:
+            flags = jnp.maximum(flags, meta_recv[q])
+        first = meta_recv[q, 0:1, 0:toks]
+        second = meta_recv[q, 1:2, 0:toks]
+        names = ((first == expert) | (second == expert)).astype(F32)
+        names = jnp.where(before(names) == wanted, names, 0.0)
+        on_list = (lax.rem(first, zs) == z) | (lax.rem(second, zs) == z)
+        on_list = jnp.broadcast_to(on_list.astype(F32), (block, toks))
+        on_list = jnp.where(before(on_list) == position, on_list, 0.0)
+        table = lax.dot_general(
+            on_list.astype(BF16), names.astype(BF16), LAST, preferred_element_type=F32
+        )
+        place_q = (same & ((wide % per_n) // SLOTS == q)).astype(F32).astype(BF16)
+        table = jnp.dot(table.astype(BF16), place_q, preferred_element_type=F32)
+        list_lo[q * block:(q + 1) * block, :] = jnp.where(lower, table, 0.0).astype(BF16)
+        list_hi[q * block:(q + 1) * block, :] = jnp.where(lower, 0.0, table).astype(BF16)
+    turn = eye(slots)
+    sort_x[...] = lax.dot_general(turn, list_lo[...], LAST, preferred_element_type=F32).astype(BF16)
+    sort_g[...] = lax.dot_general(turn, list_hi[...], LAST, preferred_element_type=F32).astype(BF16)
+    flag_n_send[...] = flags
+    spread(7, 0, flag_n_send, flag_n_recv, False, shared=True)
+
+    def dispatch(i, carry):
+        @pl.when(i + AHEAD < out_steps)
+        def _():
+            when(i, -AHEAD, out_segments, select)
+
+        when(i, 0, out_segments, resort)
+
+        @pl.when(i == 2)
+        def _():
+            for copy in weights:
+                copy.wait()
+
+        when(i, 2, out_segments, multiply)
+        when(i, 1, out_segments, share)
+        return carry
+
+    lax.fori_loop(0, out_steps + 2, dispatch, 0)
+
+    a = acc_a[...]
+    sig = jax.nn.sigmoid(a)
+    grad = acc_d[...] * sig
+    da[...] = (grad * acc_b[...] * (1.0 + a * (1.0 - sig))).astype(BF16)
+    db[...] = (grad * a).astype(BF16)
+
+    other = remote(8, 0, flag_s_send, flag_s_recv, sibling)
+
+    def combine_step(i, carry):
+        when(i, 0, back_segments, project)
+        when(i, 1, back_segments, add_halves)
+        when(i, 2, back_segments, unsort)
+
+        @pl.when(i == 4)
+        def _():
+            arrive(7, 0, flag_n_recv, False)
+            flags = flag_n_recv[0]
+            for m in range(1, nodes):
+                flags = jnp.maximum(flags, flag_n_recv[m])
+            flag_s_send[...] = flags
+            other.start()
+
+        when(i, 0, out_segments, release)
+        when(i, 4, back_segments, gather)
+        return carry
+
+    lax.fori_loop(0, max(back_steps + 4, out_steps, 5), combine_step, 0)
+
+    leave(6, 0, meta_recv, zs)
+    leave(7, 0, flag_n_recv, nodes)
+    other.wait()
+    flag_ref[...] = jnp.maximum(flag_s_send[2:3, 0:1], flag_s_recv[2:3, 0:1])
+
+
+def exchange(inputs, out_grad, experts, gates, gate_matrix, up_matrix, down_matrix):
+    nodes = lax.axis_size("node")
+    zs = lax.axis_size("local") // 2
+    toks, model = inputs.shape
+    hidden = gate_matrix.shape[2]
+    per_n = zs * SLOTS
+    slots = nodes * zs * SLOTS
+    block = 2 * CAP
+    listed = zs * block
+    steps = max(sum(count for count, _ in segs) for segs in (OUT_SEGMENTS, BACK_SEGMENTS))
+    vmem = pl.BlockSpec(memory_space=pltpu.VMEM)
+    hbm = pl.BlockSpec(memory_space=pl.ANY)
+    buffers = []
+    for count, width in OUT_SEGMENTS:
+        buffers += [
+            pltpu.VMEM((count, zs, block, width), BF16),
+            pltpu.VMEM((count, zs, block, width), BF16),
+            pltpu.VMEM((count, nodes, 2 * per_n, width), BF16),
+            pltpu.VMEM((count, 2, nodes, 2 * per_n, width), BF16),
+        ]
+    for count, width in BACK_SEGMENTS:
+        buffers += [
+            pltpu.VMEM((count, slots, width), F32),
+            pltpu.VMEM((count, slots, width), BF16),
+            pltpu.VMEM((count, slots, width), BF16),
+            pltpu.VMEM((count, nodes, per_n, width), BF16),
+            pltpu.VMEM((count, nodes, per_n, width), BF16),
+            pltpu.VMEM((count, zs, block, width // 2), BF16),
+            pltpu.VMEM((count, zs, block, width // 2), BF16),
+        ]
+    return pl.pallas_call(
+        functools.partial(kernel, nodes, zs, CAP),
+        out_shape=(
+            jax.ShapeDtypeStruct((toks, model), BF16),
+            jax.ShapeDtypeStruct((1, 1), jnp.int32),
+        ),
+        in_specs=[vmem] * 4 + [hbm] * 3,
+        out_specs=(vmem, vmem),
+        scratch_shapes=[
+            pltpu.VMEM((listed, toks), BF16),
+            pltpu.VMEM((listed, toks), BF16),
+            pltpu.VMEM((toks, listed), BF16),
+            pltpu.VMEM((toks, listed), BF16),
+            pltpu.VMEM((slots, listed), BF16),
+            pltpu.VMEM((slots, listed), BF16),
+            pltpu.VMEM((listed, slots), BF16),
+            pltpu.VMEM((listed, slots), BF16),
+            pltpu.VMEM((model, hidden), BF16),
+            pltpu.VMEM((model, hidden), BF16),
+            pltpu.VMEM((hidden, model), BF16),
+            pltpu.VMEM((2 * slots, hidden), F32),
+            pltpu.VMEM((2 * slots, hidden), F32),
+            pltpu.VMEM((2 * slots, hidden), F32),
+            pltpu.VMEM((2 * slots, hidden), BF16),
+            pltpu.VMEM((2 * slots, hidden), BF16),
+            pltpu.VMEM((8, 128), jnp.int32),
+            pltpu.VMEM((zs, 8, 128), jnp.int32),
+            pltpu.VMEM((8, 128), jnp.int32),
+            pltpu.VMEM((nodes, 8, 128), jnp.int32),
+            pltpu.VMEM((8, 128), jnp.int32),
+            pltpu.VMEM((8, 128), jnp.int32),
+            pltpu.SemaphoreType.DMA((3,)),
+            pltpu.SemaphoreType.DMA((9, steps)),
+            pltpu.SemaphoreType.DMA((9, steps)),
+            pltpu.SemaphoreType.DMA((9, steps)),
+        ] + buffers,
+        compiler_params=pltpu.CompilerParams(
+            collective_id=0, has_side_effects=True, vmem_limit_bytes=60 * 1024 * 1024
+        ),
+        name="experts_backward",
+    )(inputs, out_grad, experts, gates, gate_matrix, up_matrix, down_matrix)
 
 
 def expert_rows(x_slots, grad_slots, gate_slots, gate_matrix, up_matrix, down_matrix):
@@ -31,13 +435,13 @@
     return result.astype(jnp.bfloat16).reshape(layout)
 
 
-def shards(inputs, out_grad, experts, gate_values, gate_matrix, up_matrix, down_matrix):
+def padded(inputs, out_grad, experts, gate_values, gate_matrix, up_matrix, down_matrix):
     node_count = lax.axis_size("node")
     local_count = lax.axis_size("local")
     per_node = local_count // 2
     tok_count, model_width = inputs.shape
     expert_count = node_count * per_node
-    node_cap = min(tok_count, 2 * tok_count * NODES_TOK // node_count)
+    node_cap = min(tok_count, 2 * tok_count * 1 // node_count)
     slot_cap = 2 * node_cap // per_node
     expert_hits = experts[:, :, None] == jnp.arange(expert_count, dtype=jnp.int32)
     routed = jnp.any(expert_hits, axis=1).astype(jnp.int32)
@@ -86,15 +490,19 @@
     return total.astype(jnp.bfloat16)
 
 
+def shards(inputs, out_grad, experts, gate_values, gate_matrix, up_matrix, down_matrix):
+    weights = (gate_matrix, up_matrix, down_matrix)
+    result, flag = exchange(inputs, out_grad, experts.T, gate_values.T, *weights)
+    return lax.cond(
+        flag[0, 0] > 0,
+        lambda: padded(inputs, out_grad, experts, gate_values, *weights),
+        lambda: result,
+    )
+
+
 def solution(mesh):
-    in_specs = (
-        P(("node", "local"), None),
-        P(("node", "local"), None),
-        P(("node", "local"), None),
-        P(("node", "local"), None),
-        P(("node", "local"), None, None),
-        P(("node", "local"), None, None),
-        P(("node", "local"), None, None),
-    )
-    out_specs = P(("node", "local"), None)
-    return jax.shard_map(shards, mesh=mesh, in_specs=in_specs, out_specs=out_specs, check_vma=False)
+    rows = P(("node", "local"), None)
+    stack = P(("node", "local"), None, None)
+    return jax.shard_map(
+        shards, mesh=mesh, in_specs=(rows,) * 4 + (stack,) * 3, out_specs=rows, check_vma=False
+    )

time: 561 us -> 132 us (0.24); the launches traced: 553 us -> 132 us
  waiting for transfers between devices: 299 us -> 0 us
  Pallas kernels: 0 us -> 130 us
  blocking collectives: 104 us -> 0 us
  local copies, waits for them, and re-layouts: 76.8 us -> 0.79 us
  starting transfers between devices: 37.5 us -> 0 us
  matrix products: 33.3 us -> 0 us
    all_to_all x6 -> x0, waiting for transfers between devices: 299 us -> none  [the longest x1 75.2 us: shards(): lax.all_to_all(grad_slots, 'local', split_axis=1, concat_axis=1, tiled=True)]
    pallas_call x0 -> x1, Pallas kernels: none -> 130 us  [exchange(): pl.pallas_call(functools.partial(kernel, nodes, zs, CAP), out_shape=(jax....]
    all_to_all x2 -> x0, blocking collectives: 104 us -> none  [the longest x1 90.2 us: shards(): lax.all_to_all(partials, 'local', split_axis=1, concat_axis=1, tiled=True)]
    all_to_all x6 -> x0, starting transfers between devices: 37.5 us -> none  [the longest x1 10.6 us: shards(): lax.all_to_all(gate_slot, 'local', split_axis=1, concat_axis=1, tiled=True)]
    reshape x9 -> x0, local copies, waits for them, and re-layouts: 34.5 us -> none  [the longest x2 13.5 us: expert_rows(): return result.astype(jnp.bfloat16).reshape(layout)]
    all_to_all x7 -> x0, local copies, waits for them, and re-layouts: 33.7 us -> none  [the longest x1 7.32 us: shards(): lax.all_to_all(grad_slots, 'local', split_axis=1, concat_axis=1, tiled=True)]
    dot_general x7 -> x0, matrix products: 33.3 us -> none  [the longest x1 11.3 us: expert_rows(): lax.dot_general(grad_gate, w_gate, contract_last, preferred_element_type=...]
    broadcast_in_dim x4 -> x0, local copies, waits for them, and re-layouts: 8.13 us -> none  [the longest x1 4.06 us: shards(): jnp.repeat(x_slots.reshape(node_count, per_node, slot_cap, model_width),...]
  transfers between devices with their start and end apart: 6 -> 0, of which waited for: 6 -> 0; matrix products, arithmetic and copies ran while one was open for 7% -> 0% of each run, Pallas kernels for 0% -> 0%
where the time goes in v3:
time: 132 us
  Pallas kernels  130 us (98%)
    pallas_call x1, Pallas kernels, exchange(): pl.pallas_call(functools.partial(kernel, nodes, zs, CAP), out_shape=(jax....  130 us

profile of v3, /device:TPU:1, one launch (start us, length us, event | category | flops | bytes accessed | tf_op | source)
XLA Modules:
  0.0 131.9 jit_solution(5297039235453885845)
XLA Ops:
  0.0 0.0 copy-start.2
  0.0 0.0 copy-start.3
  0.0 0.0 copy-start.4
  0.0 0.0 copy-start.5
  0.0 130.3 %experts_backward.1 = (bf16[64,3584]{1,0:T(8,128)(2,1)S(1)}, s32[1,1]{1,0:T(1,128)}) custom-call(bf16[64,3584]{1,0:T(8,128)(2,1)} %x_ref.1, bf16[64,3584]{1,0:T(8,128)(2,1)} %g_ref.1, s32[2,64]{1,0:T(2,128)} %bitcast.68, bf16[2,64]{1,0:T(2,128)(2,1)} %bitcast.69, bf16[1,3584,512]{2,1,0:T(8,128)(2,1)} %wg_hbm.1, bf16[1,3584,512]{2,1,0:T(8,128)(2,1)} %wu_hbm.1, ...), custom_call_target="tpu_custom_call" | custom-call | tf_op jit(solution)/shard_map/experts_backward/pallas_call | solution.py:370
  130.9 0.0 copy-done.2
  130.9 0.0 copy-done.3
  130.9 0.0 copy-done.4
  130.9 0.0 copy-done.5
  130.9 0.2 conditional.1
  131.1 0.8 copy.97
Async XLA Ops:
  0.0 130.9 %copy-start.2 = (bf16[64,3584]{1,0:T(8,128)(2,1)S(1)}, bf16[64,3584]{1,0:T(8,128)(2,1)}, u32[]{:S(2)}) copy-start(bf16[64,3584]{1,0:T(8,128)(2,1)} %x_ref.1) | copy-start | bytes 1376260
  0.0 130.9 %copy-start.3 = (bf16[64,3584]{1,0:T(8,128)(2,1)S(1)}, bf16[64,3584]{1,0:T(8,128)(2,1)}, u32[]{:S(2)}) copy-start(bf16[64,3584]{1,0:T(8,128)(2,1)} %g_ref.1) | copy-start | bytes 1376260
  0.0 130.9 %copy-start.4 = (s32[64,2]{0,1:T(2,128)S(1)}, s32[64,2]{0,1:T(2,128)}, u32[]{:S(2)}) copy-start(s32[64,2]{0,1:T(2,128)} %param.11) | copy-start | bytes 1540
  0.0 130.9 %copy-start.5 = (bf16[64,2]{0,1:T(2,128)(2,1)S(1)}, bf16[64,2]{0,1:T(2,128)(2,1)}, u32[]{:S(2)}) copy-start(bf16[64,2]{0,1:T(2,128)(2,1)} %param.12) | copy-start | bytes 772

commit v4 on v3

--- a/solution.py
+++ b/solution.py
@@ -1,4 +1,5 @@
 import functools
+import math
 
 import jax
 import jax.numpy as jnp
@@ -9,9 +10,11 @@
 
 SLOTS = 2
 CAP = 24
-OUT_SEGMENTS = ((5, 512), (2, 256), (4, 128))
-BACK_SEGMENTS = ((1, 256), (6, 512), (1, 256))
-AHEAD = 2
+OUT_SEGMENTS = ((14, 256),)
+BACK_SEGMENTS = ((7, 512),)
+AHEAD = 4
+GROUP = 1
+GATHER_LAG = 4
 MESH = pl.DeviceIdType.MESH
 LAST = (((1,), (1,)), ((), ()))
 F32 = jnp.float32
@@ -56,11 +59,12 @@
 
 def kernel(
     nodes, zs, cap,
-    x_ref, g_ref, exp_ref, gate_ref, wg_hbm, wu_hbm, wd_hbm, out_ref, flag_ref,
+    x_hbm, g_hbm, exp_ref, gate_ref, wg_hbm, wu_hbm, wd_hbm, out_hbm, flag_ref,
+    x_ref, g_ref, out_ref,
     pick_x, pick_g, comb_lo, comb_hi, sort_x, sort_g, list_lo, list_hi,
     wg, wu, wd, acc_a, acc_b, acc_d, da, db,
     meta_send, meta_recv, flag_n_send, flag_n_recv, flag_s_send, flag_s_recv,
-    w_sem, send_sem, recv_sem, local_sem, *rest,
+    w_sem, send_sem, recv_sem, local_sem, out_sem, *rest,
 ):
     z_send, z_recv, n_send, n_recv = range(4)
     own, half_send, half_recv, back_send, back_recv, home_send, home_recv = range(7)
@@ -71,12 +75,25 @@
     z = local // 2
     core = local % 2
     sibling = (node, z * 2 + (1 - core))
-    toks = x_ref.shape[0]
+    toks = x_hbm.shape[0]
     per_n = zs * SLOTS
     slots = nodes * zs * SLOTS
     block = 2 * cap
     listed = zs * block
 
+    side = math.isqrt(nodes)
+    z_steps = sorted(range(1, zs), key=lambda j: (-min(j, zs - j), j))
+    node_steps = sorted(
+        ((a, b) for a in range(side) for b in range(side) if a or b),
+        key=lambda s: (-min(s[0], side - s[0]) - min(s[1], side - s[1]), s),
+    )
+
+    tokens = [
+        pltpu.make_async_copy(src, dst, w_sem.at[3 + i])
+        for i, (src, dst) in enumerate(((x_hbm, x_ref), (g_hbm, g_ref)))
+    ]
+    for copy in tokens:
+        copy.start()
     weights = [
         pltpu.make_async_copy(src.at[0], dst, w_sem.at[i])
         for i, (src, dst) in enumerate(((wg_hbm, wg), (wu_hbm, wu), (wd_hbm, wd)))
@@ -132,9 +149,13 @@
         here, count = (z, zs) if along_z else (node, nodes)
         mine = src if shared else src.at[here]
         pltpu.make_async_copy(mine, dst.at[here], local_sem.at[phase, k]).start()
-        for j in range(1, count):
-            to = lax.rem(here + j, count)
-            device = (node, to * 2 + core) if along_z else (to, local)
+        for step in z_steps if along_z else node_steps:
+            if along_z:
+                to = lax.rem(z + step, zs)
+                device = (node, to * 2 + core)
+            else:
+                to = lax.rem(node // side + step[0], side) * side + lax.rem(node % side + step[1], side)
+                device = (to, local)
             remote(phase, k, src if shared else src.at[to], dst.at[here], device).start()
 
     def arrive(phase, k, dst, along_z):
@@ -170,14 +191,29 @@
         arrive(1, c.sem, c.at(n_recv, 0), False)
         to_sibling(c).start()
 
-    def multiply(c):
-        to_sibling(c).wait_recv()
-        cols = c.columns()
-        rows = c.buffers[n_recv][c.k, :, :, 0:per_n, :].reshape(2 * slots, c.width)
+    def multiply(segment, k):
+        group = [Chunk(segment, k + n) for n in range(GROUP)]
+        for c in group:
+            to_sibling(c).wait_recv()
+        width = segment[1]
+        start = segment[2] + k * width
+        cols = pl.ds(pl.multiple_of(start, 128), GROUP * width)
+
+        def joined(part):
+            return jnp.concatenate(
+                [
+                    c.buffers[n_recv][c.k, :, :, part * per_n:(part + 1) * per_n, :].reshape(
+                        2 * slots, width
+                    )
+                    for c in group
+                ],
+                axis=1,
+            )
+
+        rows = joined(0)
         acc_a[...] += jnp.dot(rows, wg[cols, :], preferred_element_type=F32)
         acc_b[...] += jnp.dot(rows, wu[cols, :], preferred_element_type=F32)
-        rows = c.buffers[n_recv][c.k, :, :, per_n:2 * per_n, :].reshape(2 * slots, c.width)
-        acc_d[...] += lax.dot_general(rows, wd[:, cols], LAST, preferred_element_type=F32)
+        acc_d[...] += lax.dot_general(joined(1), wd[:, cols], LAST, preferred_element_type=F32)
 
     def release(c):
         leave(0, c.sem, c.at(z_recv), zs)
@@ -224,7 +260,14 @@
             out_ref[:, c.columns(h, 2)] = jnp.dot(
                 ref[...], rows, preferred_element_type=F32
             ).astype(BF16)
+        result(c).start()
         leave(5, c.sem, c.at(home_recv), zs)
+
+    def result(c):
+        cols = c.columns()
+        return pltpu.make_async_copy(
+            out_ref.at[:, cols], out_hbm.at[:, cols], out_sem.at[c.sem]
+        )
 
     def when(i, lag, segments, stage):
         for segment, count in segments:
@@ -236,6 +279,8 @@
 
     pl.semaphore_wait(barrier, zs + nodes - 1)
     spread(6, 0, meta_send, meta_recv, True, shared=True)
+    for copy in tokens:
+        copy.wait()
     early = [Chunk(segment, k) for segment, count in out_segments for k in range(count)][:AHEAD]
     for c in early:
         select(c)
@@ -297,7 +342,13 @@
             for copy in weights:
                 copy.wait()
 
-        when(i, 2, out_segments, multiply)
+        for segment, count in out_segments:
+            start = segment[3] + GROUP + 1
+
+            @pl.when((i >= start) & (i < start + count) & ((i - start) % GROUP == 0))
+            def _():
+                multiply(segment, i - start)
+
         when(i, 1, out_segments, share)
         return carry
 
@@ -326,10 +377,11 @@
             other.start()
 
         when(i, 0, out_segments, release)
-        when(i, 4, back_segments, gather)
+        when(i, GATHER_LAG, back_segments, gather)
+        when(i, GATHER_LAG + 1, back_segments, lambda c: result(c).wait())
         return carry
 
-    lax.fori_loop(0, max(back_steps + 4, out_steps, 5), combine_step, 0)
+    lax.fori_loop(0, max(back_steps + GATHER_LAG + 1, out_steps, 5), combine_step, 0)
 
     leave(6, 0, meta_recv, zs)
     leave(7, 0, flag_n_recv, nodes)
@@ -373,9 +425,12 @@
             jax.ShapeDtypeStruct((toks, model), BF16),
             jax.ShapeDtypeStruct((1, 1), jnp.int32),
         ),
-        in_specs=[vmem] * 4 + [hbm] * 3,
-        out_specs=(vmem, vmem),
+        in_specs=[hbm] * 2 + [vmem] * 2 + [hbm] * 3,
+        out_specs=(hbm, vmem),
         scratch_shapes=[
+            pltpu.VMEM((toks, model), BF16),
+            pltpu.VMEM((toks, model), BF16),
+            pltpu.VMEM((toks, model), BF16),
             pltpu.VMEM((listed, toks), BF16),
             pltpu.VMEM((listed, toks), BF16),
             pltpu.VMEM((toks, listed), BF16),
@@ -398,10 +453,11 @@
             pltpu.VMEM((nodes, 8, 128), jnp.int32),
             pltpu.VMEM((8, 128), jnp.int32),
             pltpu.VMEM((8, 128), jnp.int32),
-            pltpu.SemaphoreType.DMA((3,)),
+            pltpu.SemaphoreType.DMA((5,)),
             pltpu.SemaphoreType.DMA((9, steps)),
             pltpu.SemaphoreType.DMA((9, steps)),
             pltpu.SemaphoreType.DMA((9, steps)),
+            pltpu.SemaphoreType.DMA((steps,)),
         ] + buffers,
         compiler_params=pltpu.CompilerParams(
             collective_id=0, has_side_effects=True, vmem_limit_bytes=60 * 1024 * 1024

time: 132 us -> 126 us (0.955)
  Pallas kernels: 130 us -> 125 us
    pallas_call x1, Pallas kernels: 130 us -> 125 us  [exchange(): pl.pallas_call(functools.partial(kernel, nodes, zs, CAP), out_shape=(jax....]
where the time goes in v4:
time: 126 us
  Pallas kernels  125 us (99%)
    pallas_call x1, Pallas kernels, exchange(): pl.pallas_call(functools.partial(kernel, nodes, zs, CAP), out_shape=(jax....  125 us

profile of v4, /device:TPU:1, one launch (start us, length us, event | category | flops | bytes accessed | tf_op | source)
XLA Modules:
  0.0 126.2 jit_solution(12254293928647390661)
XLA Ops:
  0.0 0.0 copy-start.2
  0.0 0.0 copy-start.3
  0.0 0.0 copy-start.4
  0.0 0.0 copy-start.5
  0.0 124.6 %experts_backward.1 = (bf16[64,3584]{1,0:T(8,128)(2,1)S(1)}, s32[1,1]{1,0:T(1,128)}) custom-call(bf16[64,3584]{1,0:T(8,128)(2,1)} %x_hbm.1, bf16[64,3584]{1,0:T(8,128)(2,1)} %g_hbm.1, s32[2,64]{1,0:T(2,128)} %bitcast.68, bf16[2,64]{1,0:T(2,128)(2,1)} %bitcast.69, bf16[1,3584,512]{2,1,0:T(8,128)(2,1)} %wg_hbm.1, bf16[1,3584,512]{2,1,0:T(8,128)(2,1)} %wu_hbm.1, ...), custom_call_target="tpu_custom_call" | custom-call | tf_op jit(solution)/shard_map/experts_backward/pallas_call | solution.py:422
  125.2 0.0 copy-done.2
  125.2 0.0 copy-done.3
  125.2 0.0 copy-done.4
  125.2 0.0 copy-done.5
  125.2 0.2 conditional.1
  125.5 0.8 copy.97
Async XLA Ops:
  0.0 125.2 %copy-start.2 = (bf16[64,3584]{1,0:T(8,128)(2,1)S(1)}, bf16[64,3584]{1,0:T(8,128)(2,1)}, u32[]{:S(2)}) copy-start(bf16[64,3584]{1,0:T(8,128)(2,1)} %x_hbm.1) | copy-start | bytes 1376260
  0.0 125.2 %copy-start.3 = (bf16[64,3584]{1,0:T(8,128)(2,1)S(1)}, bf16[64,3584]{1,0:T(8,128)(2,1)}, u32[]{:S(2)}) copy-start(bf16[64,3584]{1,0:T(8,128)(2,1)} %g_hbm.1) | copy-start | bytes 1376260
  0.0 125.2 %copy-start.4 = (s32[64,2]{0,1:T(2,128)S(1)}, s32[64,2]{0,1:T(2,128)}, u32[]{:S(2)}) copy-start(s32[64,2]{0,1:T(2,128)} %param.11) | copy-start | bytes 1540
  0.0 125.2 %copy-start.5 = (bf16[64,2]{0,1:T(2,128)(2,1)S(1)}, bf16[64,2]{0,1:T(2,128)(2,1)}, u32[]{:S(2)}) copy-start(bf16[64,2]{0,1:T(2,128)(2,1)} %param.12) | copy-start | bytes 772
